TPU v7x, 32 devices: a whole 2x2x4 slice. The times are simulated.
32 devices in a mesh: groups: 2 (over y), dp: 4 (over z), tensor: 4 (over x, core).
Axes of the slice: x: 2, y: 2, z: 4, core: 2. Of those that a mesh axis runs over, the one named last changes fastest.
Arguments:
- tiles: bfloat16 [32, 256, 588], P(('groups', 'dp'), 'tensor'), parts along dimension 0, may hold values from -6 to 6
- tile_index: int32 [32], P(('groups', 'dp')), parts along dimension 0, may hold values from 0 to 3
- tile_from: int32 [16], P('groups'), parts along dimension 0, may hold values from 0 to 15, as said below
- patch_weight: bfloat16 [588, 1280], P(None, 'tensor'), may hold values from -0.25 to 0.25
- tile_table: float32 [4, 1280], replicated, may hold values from -3 to 3
- ln1_gain: float32 [1280], replicated, may hold values from 0.25 to 1.75
- ln1_bias: float32 [1280], replicated, may hold values from -1.5 to 1.5
- qkv_weight: bfloat16 [1280, 3, 1280], P(None, None, 'tensor'), may hold values from -32 to 32
- out_weight: bfloat16 [1280, 1280], P('tensor'), may hold values from -0.15625 to 0.15625
- ln2_gain: float32 [1280], replicated, may hold values from 0.25 to 1.75
- ln2_bias: float32 [1280], replicated, may hold values from -1.5 to 1.5
- fc1_weight: bfloat16 [1280, 5120], P(None, 'tensor'), may hold values from -0.15625 to 0.15625
- fc1_bias: float32 [5120], P('tensor'), may hold values from -1.5 to 1.5
- fc2_weight: bfloat16 [5120, 1280], P('tensor'), may hold values from -0.078125 to 0.078125
- fc2_bias: float32 [1280], replicated, may hold values from -1.5 to 1.5
- ln3_gain: float32 [1280], replicated, may hold values from 0.25 to 1.75
- ln3_bias: float32 [1280], replicated, may hold values from -1.5 to 1.5
- kv_weight: bfloat16 [1280, 2, 1024], P(None, None, 'tensor'), may hold values from -0.15625 to 0.15625
- knorm_gain: float32 [128], replicated, may hold values from 0.25 to 1.75
- page_owner: int32 [256], P(('groups', 'dp')), parts along dimension 0, may hold values from 0 to 3, as said below
- page_slot: int32 [256], P(('groups', 'dp')), parts along dimension 0, may hold values from 0 to 63, as said below
Outputs:
- cache: bfloat16 [512, 16, 2, 1024], P(('groups', 'dp'), None, None, 'tensor'), parts along dimension 0
There are 2 independent parts, one for each index of `groups`. A program takes and returns all parts, laid end to end along the dimension named above; an argument that names none is the same for every part. Nothing has to cross between parts.
Inputs may be any that keep to these rules, and one draw needn't show every extreme that they name: `tile_from`: entry r * 2 + s names, as src * 4 + slot, the held tile that rank r encodes in its slot s. Every named tile is named once. A rank that encodes its own tile keeps it in place (s = slot < 2); a tile that changes rank comes from a slot 2 or higher. No rank hands more than 1 tiles to one other rank, and some pair reaches it; some rank holds 4 named tiles. Slots that are not named hold no work. `page_owner`: of the 32 pages of one rank at most 16 go to one owner, and some owner receives exactly 16 from every rank; no owner receives more than 64 pages. `page_slot`: pages with the same owner have different slots.
All inputs are finite; a program needn't handle non-finite values.
Results may differ from a plain program's by a relative error of at most 0.014.
Values may be sent and summed in bfloat16 or wider, within the bound.
A program may use at most 128 MiB of HBM per device.

v0:
```python
import jax
import jax.numpy as jnp
from jax import lax
from jax.sharding import PartitionSpec as P

HEAD_DIM = 80
KV_DIM = 128
PAGE = 16


def layer_norm(values, gain, bias):
    mean = jnp.mean(values, axis=-1, keepdims=True)
    centred = values - mean
    spread = jnp.mean(centred * centred, axis=-1, keepdims=True)
    return (centred * lax.rsqrt(spread + 1e-05) * gain + bias).astype(jnp.bfloat16)


def on_device(
    tiles,
    tile_index,
    tile_from,
    patch_weight,
    tile_table,
    ln1_gain,
    ln1_bias,
    qkv_weight,
    out_weight,
    ln2_gain,
    ln2_bias,
    fc1_weight,
    fc1_bias,
    fc2_weight,
    fc2_bias,
    ln3_gain,
    ln3_bias,
    kv_weight,
    knorm_gain,
    page_owner,
    page_slot,
):
    ranks = lax.axis_size("dp")
    rank_here = lax.axis_index("dp")
    holding = tiles.shape[0]
    balanced = tile_from.shape[0] // ranks
    wanted = lax.dynamic_slice_in_dim(tile_from, rank_here * balanced, balanced)
    wanted_source = wanted // holding
    wanted_anchor = wanted % holding
    arrived, arrived_index = (
        lax.all_gather(tiles[balanced:], "dp", axis=0, tiled=True),
        lax.all_gather(tile_index[balanced:], "dp", axis=0, tiled=True),
    )
    pick_row = jnp.where(
        wanted_source == rank_here,
        wanted_anchor,
        holding + wanted_source * balanced + wanted_anchor - balanced,
    )
    pixels = jnp.take(jnp.concatenate([tiles, arrived], axis=0), pick_row, axis=0)
    work_index = jnp.take(jnp.concatenate([tile_index, arrived_index], axis=0), pick_row, axis=0)
    pixels = jnp.swapaxes(pixels, 0, 1)
    full_patch = lax.all_gather(patch_weight, "tensor", axis=1, tiled=True)
    embedded = jnp.einsum(
        "tbp,pc->tbc", pixels, full_patch, preferred_element_type=jnp.float32
    ).astype(jnp.bfloat16)
    choose = (
        work_index[:, None] == jnp.arange(tile_table.shape[0], dtype=jnp.int32)[None, :]
    ).astype(jnp.float32)
    position_rows = jnp.sum(choose[:, :, None] * tile_table[None, :, :], axis=1)
    state = embedded.astype(jnp.float32) + position_rows[None, :, :]
    normed = layer_norm(state, ln1_gain, ln1_bias)
    joint_weight = qkv_weight.reshape(qkv_weight.shape[0], -1)
    projected = jnp.einsum(
        "tbd,dc->tbc",
        lax.all_gather(normed, "tensor", axis=0, tiled=True),
        joint_weight,
        preferred_element_type=jnp.float32,
    ).astype(jnp.bfloat16)
    tile_length = projected.shape[0]
    heads_here = qkv_weight.shape[2] // HEAD_DIM
    projected = projected.reshape(tile_length, balanced, 3, heads_here, HEAD_DIM)
    scores = jnp.einsum(
        "qbhd,kbhd->bhqk",
        projected[:, :, 0],
        projected[:, :, 1],
        preferred_element_type=jnp.float32,
    ) * HEAD_DIM ** (-0.5)
    weights = jax.nn.softmax(scores, axis=-1).astype(jnp.bfloat16)
    context = jnp.einsum(
        "bhqk,kbhd->qbhd", weights, projected[:, :, 2], preferred_element_type=jnp.float32
    ).astype(jnp.bfloat16)
    context = context.reshape(tile_length, balanced, heads_here * HEAD_DIM)
    block = context
    state = state + lax.psum_scatter(
        jnp.einsum("tbc,cd->tbd", block, out_weight, preferred_element_type=jnp.float32),
        "tensor",
        scatter_dimension=0,
        tiled=True,
    )
    normed = layer_norm(state, ln2_gain, ln2_bias)
    inner = (
        jnp.einsum(
            "tbd,df->tbf",
            lax.all_gather(normed, "tensor", axis=0, tiled=True),
            fc1_weight,
            preferred_element_type=jnp.float32,
        )
        + fc1_bias
    )
    hidden = jax.nn.gelu(inner, approximate=False).astype(jnp.bfloat16)
    block = hidden
    state = (
        state
        + lax.psum_scatter(
            jnp.einsum("tbf,fd->tbd", block, fc2_weight, preferred_element_type=jnp.float32),
            "tensor",
            scatter_dimension=0,
            tiled=True,
        )
        + fc2_bias
    )
    normed = layer_norm(state, ln3_gain, ln3_bias)
    piece = lax.all_gather(normed, "tensor", axis=0, tiled=True)
    both = jnp.einsum("tbd,dkc->tbkc", piece, kv_weight, preferred_element_type=jnp.float32)
    row_count = piece.shape[0]
    tiles_here = piece.shape[1]
    keys = both[:, :, 0].reshape(row_count, tiles_here, -1, KV_DIM)
    keys = keys * lax.rsqrt(jnp.mean(keys * keys, axis=-1, keepdims=True) + 1e-05) * knorm_gain
    cached = jnp.stack([keys.reshape(row_count, tiles_here, -1), both[:, :, 1]], axis=2).astype(
        jnp.bfloat16
    )
    per_tile = tile_length // PAGE
    page_count = balanced * per_tile
    paged = cached.reshape(per_tile, PAGE, balanced, 2, cached.shape[-1])
    page_cap = max(2, 2 * ((page_count + ranks - 1) // ranks))
    numbers = jnp.arange(page_count, dtype=jnp.int32)
    earlier = (page_owner[:, None] == page_owner[None, :]) & (numbers[None, :] < numbers[:, None])
    target_place = page_owner * page_cap + jnp.sum(earlier.astype(jnp.int32), axis=1)
    places = jnp.arange(ranks * page_cap, dtype=jnp.int32)
    routed = target_place[None, :] == places[:, None]
    routing = routed.astype(jnp.bfloat16).reshape(ranks * page_cap, balanced, per_tile)
    outgoing_pages = jnp.einsum(
        "sbp,prbkc->srkc", routing, paged, preferred_element_type=jnp.float32
    ).astype(jnp.bfloat16)
    outgoing_slots = jnp.where(
        jnp.any(routed, axis=1), jnp.sum(jnp.where(routed, page_slot[None, :], 0), axis=1), -1
    )
    arrived_pages, arrived_slots = (
        lax.all_to_all(outgoing_pages, "dp", split_axis=0, concat_axis=0, tiled=True),
        lax.all_to_all(outgoing_slots, "dp", split_axis=0, concat_axis=0, tiled=True),
    )
    cache_slots = ranks * page_cap
    placing = (arrived_slots[None, :] == jnp.arange(cache_slots, dtype=jnp.int32)[:, None]).astype(
        jnp.bfloat16
    )
    return jnp.einsum(
        "ms,srkc->mrkc", placing, arrived_pages, preferred_element_type=jnp.float32
    ).astype(jnp.bfloat16)


def solution(mesh):
    return jax.shard_map(
        on_device,
        mesh=mesh,
        in_specs=(
            P(("groups", "dp"), "tensor", None),
            P(("groups", "dp")),
            P("groups"),
            P(None, "tensor"),
            P(),
            P(),
            P(),
            P(None, None, "tensor"),
            P("tensor", None),
            P(),
            P(),
            P(None, "tensor"),
            P("tensor"),
            P("tensor", None),
            P(),
            P(),
            P(),
            P(None, None, "tensor"),
            P(),
            P(("groups", "dp")),
            P(("groups", "dp")),
        ),
        out_specs=P(("groups", "dp"), None, None, "tensor"),
        check_vma=False,
    )
```

profile of v0, /device:TPU:0, one launch (start us, length us, event | category | flops | bytes accessed | tf_op | source)
XLA Modules:
  0.0 262.7 jit_solution(4913952394533338164)
XLA Ops:
  10.2 9.9 %all-reduce = s32[8]{0:T(128)S(1)} all-reduce(s32[8]{0:T(128)S(1)} %slice_dynamic-update-slice_fusion), channel_id=1, replica_groups=mesh['groups'=2,'dp'=4,'tensor'=4] {'dp'}, use_global_device_ids=true, to_apply=%add | all-reduce | flops 8 | bytes 64
  23.2 16.5 %all_gather.18 = bf16[8,64,588]{2,1,0:T(8,128)(2,1)S(1)} all-gather(bf16[2,64,588]{2,1,0:T(8,128)(2,1)S(1)} %slice.22), channel_id=1, replica_groups=mesh['groups'=2,'dp'=4,'tensor'=4] {'dp'}, dimensions={0}, use_global_device_ids=true | all-gather | bytes 752640 | tf_op jit(solution)/shard_map/all_gather | solution.py:49
  39.6 2.1 pad_maximum_fusion
  43.7 2.1 fusion.120
  47.7 18.2 %all-gather.7.cloned.1.call-done = bf16[256,2,1280]{2,0,1:T(8,128)(2,1)} async-done(((bf16[64,2,1280]{2,0,1:T(8,128)(2,1)}), bf16[256,2,1280]{2,0,1:T(8,128)(2,1)}) %all-gather.7.cloned.1.call-update) | async-done | bytes 1310736 | tf_op jit(solution)/shard_map/all_gather | solution.py:73
  65.8 4.5 %convolution_convert_fusion.2 = bf16[256,2,960]{0,2,1:T(8,128)(2,1)} fusion(bf16[256,2,1280]{2,0,1:T(8,128)(2,1)} %all-gather.7.cloned.1.call-done, bf16[1280,960,1]{0,1,2:T(8,128)(2,1)} %bitcast.108), kind=kOutput, calls=%fused_computation.39 | convolution fusion | flops 1258782720 | bytes 4751360 | tf_op jit(solution)/shard_map/tbd,dc->tbc/dot_general | solution.py:71
  72.2 3.0 %convolution_convert_fusion.3 = bf16[2,4,80,256]{3,2,1,0:T(8,128)(2,1)} fusion(f32[2,4,256]{2,1,0:T(4,128)S(1)} %fusion.121, bf16[256,2,3,4,80]{0,4,3,2,1:T(8,128)(2,1)} %bitcast.110), kind=kOutput, calls=%fused_computation.75 | convolution fusion | flops 170035456 | bytes 1318912 | tf_op jit(solution)/shard_map/bhqk,kbhd->qbhd/dot_general | solution.py:87
  75.3 3.6 %fusion.55 = f32[256,2,1280]{2,0,1:T(8,128)} fusion(bf16[256,2,320]{0,2,1:T(8,128)(2,1)} %bitcast.107, bf16[320,1280]{1,0:T(8,128)(2,1)} %param.29), kind=kOutput, calls=%fused_computation.79 | convolution fusion | flops 419430400 | bytes 3768320 | tf_op jit(solution)/shard_map/tbc,cd->tbd/dot_general | solution.py:93
  79.0 34.7 %reduce-scatter.3.cloned.1.call-done = f32[64,2,1280]{2,0,1:T(8,128)} async-done(((f32[256,2,1280]{2,0,1:T(8,128)}), f32[64,2,1280]{2,0,1:T(8,128)}) %reduce-scatter.3.cloned.1.call-update) | async-done | bytes 655376 | tf_op jit(solution)/shard_map/reduce_scatter | solution.py:92
  117.0 18.3 %all-gather.9.cloned.1.call-done = bf16[256,2,1280]{2,0,1:T(8,128)(2,1)} async-done(((bf16[64,2,1280]{2,0,1:T(8,128)(2,1)}), bf16[256,2,1280]{2,0,1:T(8,128)(2,1)}) %all-gather.9.cloned.1.call-update) | async-done | bytes 1310736 | tf_op jit(solution)/shard_map/all_gather | solution.py:102
  135.3 3.9 %fusion.58 = (u8[256,1280]{1,0:T(8,128)(4,1)S(1)}, u8[256,1280]{1,0:T(8,128)(4,1)S(1)}, f32[256,2,1280]{2,0,1:T(8,128)S(1)}) fusion(f32[1280]{0:T(1024)S(1)} %copy-done.13, bf16[256,2,1280]{2,0,1:T(8,128)(2,1)} %all-gather.9.cloned.1.call-done, bf16[1280,1280]{1,0:T(8,128)(2,1)S(1)} %copy-done), kind=kOutput, calls=%fused_computation.89 | convolution fusion | flops 1686241280 | bytes 7869440 | tf_op jit(solution)/shard_map/tbd,df->tbf/dot_general | solution.py:100
  139.3 8.9 %fusion.1 = f32[256,2,1280]{2,0,1:T(8,128)} fusion(bf16[1280,1280]{1,0:T(8,128)(2,1)S(1)} %copy-done.12, f32[256,2,1280]{2,0,1:T(8,128)S(1)} %get-tuple-element.15, u8[256,1280]{1,0:T(8,128)(4,1)S(1)} %get-tuple-element.6, u8[256,1280]{1,0:T(8,128)(4,1)S(1)} %get-tuple-element.5), kind=kOutput, calls=%fused_computation.5 | convolution fusion | flops 1723596800 | bytes 9175040 | tf_op jit(solution)/shard_map/tbf,fd->tbd/dot_general | solution.py:113
  148.2 34.7 %reduce-scatter.5.cloned.1.call-done = f32[64,2,1280]{2,0,1:T(8,128)} async-done(((f32[256,2,1280]{2,0,1:T(8,128)}), f32[64,2,1280]{2,0,1:T(8,128)}) %reduce-scatter.5.cloned.1.call-update) | async-done | bytes 655376 | tf_op jit(solution)/shard_map/reduce_scatter | solution.py:112
  186.6 4.6 %all-to-all-start = ((s32[4,16,1]{1,2,0:T(1,128)}), s32[4,16,1]{1,2,0:T(1,128)S(1)}, u32[]{:S(2)}, u32[]{:S(2)}) async-start(s32[4,16,1]{1,2,0:T(1,128)} %bitcast), calls=%async_computation | async-start | bytes 4096 | tf_op jit(solution)/shard_map/all_to_all | solution.py:148
  191.3 12.6 %all-gather.11.cloned.1.call-done = bf16[256,2,1280]{2,0,1:T(8,128)(2,1)} async-done(((bf16[64,2,1280]{2,0,1:T(8,128)(2,1)}), bf16[256,2,1280]{2,0,1:T(8,128)(2,1)}) %all-gather.11.cloned.1.call-update) | async-done | bytes 1310736 | tf_op jit(solution)/shard_map/all_gather | solution.py:121
  203.9 2.5 fusion.19
  207.7 2.1 mul.167
  209.8 2.4 reduce_sum.109
  214.5 2.3 mul.169
  218.8 2.1 copy.78
  220.8 4.6 %all-to-all-start.1 = ((bf16[64,16,2,256]{3,2,1,0:T(2,128)(2,1)}), bf16[64,16,2,256]{3,2,1,0:T(2,128)(2,1)}, u32[]{:S(2)}, u32[]{:S(2)}) async-start(bf16[64,16,2,256]{3,2,1,0:T(2,128)(2,1)} %copy.78), calls=%async_computation.3 | async-start | bytes 2097152 | tf_op jit(solution)/shard_map/all_to_all | solution.py:147
  226.8 24.8 %all-to-all-done.1 = bf16[64,16,2,256]{3,2,1,0:T(2,128)(2,1)} async-done(((bf16[64,16,2,256]{3,2,1,0:T(2,128)(2,1)}), bf16[64,16,2,256]{3,2,1,0:T(2,128)(2,1)}, u32[]{:S(2)}, u32[]{:S(2)}) %all-to-all-start.1) | async-done | bytes 1048608 | tf_op jit(solution)/shard_map/all_to_all | solution.py:147
  251.7 2.1 convolution_convert_fusion.1
  253.8 2.1 copy.80
  (94 shorter events, 25.8 us)
Async XLA Ops:
  6.5 128.8 %copy-start = (bf16[1280,1280]{1,0:T(8,128)(2,1)S(1)}, bf16[1280,1280]{1,0:T(8,128)(2,1)}, u32[]{:S(2)}) copy-start(bf16[1280,1280]{1,0:T(8,128)(2,1)} %param.32) | copy-start | bytes 9830404
  6.5 37.0 %copy-start.4 = (f32[4,1280]{1,0:T(4,128)S(1)}, f32[4,1280]{1,0:T(4,128)}, u32[]{:S(2)}) copy-start(f32[4,1280]{1,0:T(4,128)} %param.25) | copy-start | bytes 61444
  6.5 37.1 %all-gather.5.cloned.1.call-start = ((), (), s32[]{:S(2)}) async-start(), calls=%async_computation.4 | async-start | bytes 2048000 | tf_op jit(solution)/shard_map/all_gather | solution.py:60
  7.3 58.6 %all-gather.7.cloned.1.call-start = ((), (), s32[]{:S(2)}) async-start(), calls=%async_computation.5 | async-start | bytes 1638400 | tf_op jit(solution)/shard_map/all_gather | solution.py:73
  39.6 7.1 %copy-start.5 = (f32[1280]{0:T(1024)S(1)}, f32[1280]{0:T(1024)}, u32[]{:S(2)}) copy-start(f32[1280]{0:T(1024)} %param.27) | copy-start | bytes 15364
  39.6 7.1 %copy-start.6 = (f32[1280]{0:T(1024)S(1)}, f32[1280]{0:T(1024)}, u32[]{:S(2)}) copy-start(f32[1280]{0:T(1024)} %param.26) | copy-start | bytes 15364
  45.8 0.8 copy-start.1
  47.6 66.1 %reduce-scatter.3.cloned.1.call-start = ((), (), s32[]{:S(2)}) async-start(), calls=%async_computation.6 | async-start | bytes 3276800 | tf_op jit(solution)/shard_map/reduce_scatter | solution.py:92
  78.9 37.1 %copy-start.7 = (f32[1280]{0:T(1024)S(1)}, f32[1280]{0:T(1024)}, u32[]{:S(2)}) copy-start(f32[1280]{0:T(1024)} %param.31) | copy-start | bytes 15364
  78.9 37.1 %copy-start.8 = (f32[1280]{0:T(1024)S(1)}, f32[1280]{0:T(1024)}, u32[]{:S(2)}) copy-start(f32[1280]{0:T(1024)} %param.30) | copy-start | bytes 15364
  78.9 56.4 %copy-start.13 = (f32[1280]{0:T(1024)S(1)}, f32[1280]{0:T(1024)}, u32[]{:S(2)}) copy-start(f32[1280]{0:T(1024)} %param.33) | copy-start | bytes 15364
  78.9 56.4 %all-gather.9.cloned.1.call-start = ((), (), s32[]{:S(2)}) async-start(), calls=%async_computation.7 | async-start | bytes 1638400 | tf_op jit(solution)/shard_map/all_gather | solution.py:102
  117.0 66.0 %reduce-scatter.5.cloned.1.call-start = ((), (), s32[]{:S(2)}) async-start(), calls=%async_computation.8 | async-start | bytes 3276800 | tf_op jit(solution)/shard_map/reduce_scatter | solution.py:112
  135.3 4.0 %copy-start.12 = (bf16[1280,1280]{1,0:T(8,128)(2,1)S(1)}, bf16[1280,1280]{1,0:T(8,128)(2,1)}, u32[]{:S(2)}) copy-start(bf16[1280,1280]{1,0:T(8,128)(2,1)} %param.34) | copy-start | bytes 9830404
  148.1 34.8 %copy-start.9 = (f32[1280]{0:T(1024)S(1)}, f32[1280]{0:T(1024)}, u32[]{:S(2)}) copy-start(f32[1280]{0:T(1024)} %param.35) | copy-start | bytes 15364
  148.1 36.5 %copy-start.10 = (f32[1280]{0:T(1024)S(1)}, f32[1280]{0:T(1024)}, u32[]{:S(2)}) copy-start(f32[1280]{0:T(1024)} %param.37) | copy-start | bytes 15364
  148.1 36.5 %copy-start.11 = (f32[1280]{0:T(1024)S(1)}, f32[1280]{0:T(1024)}, u32[]{:S(2)}) copy-start(f32[1280]{0:T(1024)} %param.36) | copy-start | bytes 15364
  148.2 37.4 %copy-start.14 = (s32[32]{0:T(128)S(1)}, s32[32]{0:T(128)}, u32[]{:S(2)}) copy-start(s32[32]{0:T(128)} %param.40) | copy-start | bytes 388
  148.2 37.7 %copy-start.15 = (s32[32]{0:T(128)S(1)}, s32[32]{0:T(128)}, u32[]{:S(2)}) copy-start(s32[32]{0:T(128)} %param.41) | copy-start | bytes 388
  148.2 43.1 %copy-start.16 = (f32[128]{0:T(128)S(1)}, f32[128]{0:T(128)}, u32[]{:S(2)}) copy-start(f32[128]{0:T(128)} %param.39) | copy-start | bytes 1540
  148.2 55.7 %all-gather.11.cloned.1.call-start = ((), (), s32[]{:S(2)}) async-start(), calls=%async_computation.9 | async-start | bytes 1638400 | tf_op jit(solution)/shard_map/all_gather | solution.py:121
  186.6 34.2 %all-to-all-start = ((s32[4,16,1]{1,2,0:T(1,128)}), s32[4,16,1]{1,2,0:T(1,128)S(1)}, u32[]{:S(2)}, u32[]{:S(2)}) async-start(s32[4,16,1]{1,2,0:T(1,128)} %bitcast), calls=%async_computation | async-start | bytes 4096 | tf_op jit(solution)/shard_map/all_to_all | solution.py:148
  206.5 1.1 copy-start.3
  220.8 30.8 %all-to-all-start.1 = ((bf16[64,16,2,256]{3,2,1,0:T(2,128)(2,1)}), bf16[64,16,2,256]{3,2,1,0:T(2,128)(2,1)}, u32[]{:S(2)}, u32[]{:S(2)}) async-start(bf16[64,16,2,256]{3,2,1,0:T(2,128)(2,1)} %copy.78), calls=%async_computation.3 | async-start | bytes 2097152 | tf_op jit(solution)/shard_map/all_to_all | solution.py:147
  (1 other events, 0.8 us)
Sparse Core Ops, SparseCore 0:
  8.9 22.7 all-gather.4
  47.7 18.0 all-gather.6
  79.0 34.6 reduce-scatter.2
  117.1 18.1 all-gather.8
  148.3 34.6 reduce-scatter.4
  185.7 18.1 all-gather.10
where the time goes:
time: 263 us
  waiting for transfers between devices  144 us (55%)
  matrix products  33.2 us (13%)
  blocking collectives  26.3 us (10%)
  local copies, waits for them, and re-layouts  18.5 us (7%)
  other arithmetic  16.7 us (6%)
  between operations  14.4 us (5%)
  starting transfers between devices  9.42 us (4%)
    all_gather x2, waiting for transfers between devices, on_device(): lax.all_gather(normed, 'tensor', axis=0, tiled=True)  36.5 us
    reduce_scatter x1, waiting for transfers between devices, on_device(): lax.psum_scatter(jnp.einsum('tbc,cd->tbd', block, out_weight, preferred_e...  34.7 us
    reduce_scatter x1, waiting for transfers between devices, on_device(): lax.psum_scatter(jnp.einsum('tbf,fd->tbd', block, fc2_weight, preferred_e...  34.7 us
    all_to_all x1, waiting for transfers between devices, on_device(): lax.all_to_all(outgoing_pages, 'dp', split_axis=0, concat_axis=0, tiled=T...  24.8 us
    all_gather x1, blocking collectives, on_device(): lax.all_gather(tiles[balanced:], 'dp', axis=0, tiled=True)  16.5 us
    all_gather x1, waiting for transfers between devices, on_device(): piece = lax.all_gather(normed, 'tensor', axis=0, tiled=True)  12.6 us
    unnamed x1, blocking collectives  9.89 us
    dot_general x1, matrix products, on_device(): jnp.einsum('tbf,fd->tbd', block, fc2_weight, preferred_element_type=jnp.f...  8.86 us
  transfers between devices with their start and end apart: 8, of which 6 were waited for; matrix products, arithmetic and copies ran while one was open for 11% of the time, Pallas kernels for 0%

commit v1 on v0

v1 whole, which is shorter than its diff:
```python
import functools

import jax
import jax.numpy as jnp
from jax import lax
from jax.experimental import pallas as pl
from jax.experimental.pallas import tpu as pltpu
from jax.sharding import PartitionSpec as P

HEAD_DIM = 80
KV_DIM = 128
PAGE = 16
CHUNKS = 4
F32 = jnp.float32
BF16 = jnp.bfloat16


def normalise(x, gain, bias):
    mean = jnp.mean(x, axis=-1, keepdims=True)
    centred = x - mean
    spread = jnp.mean(centred * centred, axis=-1, keepdims=True)
    return (centred * lax.rsqrt(spread + 1e-05) * gain + bias).astype(BF16)


def dot(a, b):
    return jnp.dot(a, b, preferred_element_type=F32)


def dot_t(a, b):
    return lax.dot_general(a, b, (((1,), (1,)), ((), ())), preferred_element_type=F32)


def wide(total):
    return 256 if total % 256 == 0 else total


def kernel(
    ranks,
    cap,
    from_ref,
    order_ref,
    ints_ref,
    tiles_ref,
    patch_ref,
    table_ref,
    g1_ref,
    b1_ref,
    g2_ref,
    b2_ref,
    g3_ref,
    b3_ref,
    fb1_ref,
    fb2_ref,
    kg_ref,
    wq_hbm,
    wk_hbm,
    wv_hbm,
    wo_hbm,
    w1_hbm,
    w2_hbm,
    wkv_hbm,
    out_ref,
    wq,
    wk,
    wv,
    wo,
    w1,
    w2,
    wkv,
    patch,
    ints_in,
    tile_out,
    tile_in,
    pix,
    state,
    n1,
    n2,
    n3,
    q_s,
    k_s,
    v_s,
    ctx,
    hid,
    acc,
    sib_out,
    sib_in,
    x_out,
    x_in,
    kvp,
    page_out,
    page_in,
    source_v,
    source_s,
    wsem,
    ints_sem,
    tile_sem,
    page_sem,
    patch_sem,
    pix_sem,
    sib_sem,
    x_sem,
    n_sem,
    s_sem,
):
    me = lax.axis_index("dp")
    t = lax.axis_index("tensor")
    core = lax.rem(t, 2)
    other = 1 - core
    sib = t + 1 - 2 * core
    far = lax.rem(t + 2, 4)
    far_sib = lax.rem(sib + 2, 4)
    hold, toks, width = tiles_ref.shape
    balanced = from_ref.shape[0] // ranks
    length = state.shape[0]
    dim = state.shape[1]
    rows = length // CHUNKS
    local_cols = wq.shape[1]
    heads = local_cols // HEAD_DIM

    weights = [
        (wq_hbm, wq),
        (wk_hbm, wk),
        (wv_hbm, wv),
        (wo_hbm, wo),
        (w1_hbm, w1),
        (w2_hbm, w2),
        (wkv_hbm, wkv),
    ]
    loads = [pltpu.make_async_copy(a, b, wsem.at[i]) for i, (a, b) in enumerate(weights)]
    for load in loads:
        load.start()

    barrier = pltpu.get_barrier_semaphore()
    for peer in (sib, far):
        pl.semaphore_signal(barrier, inc=1, device_id={"tensor": peer})
    for k in range(1, ranks):
        pl.semaphore_signal(barrier, inc=1, device_id={"dp": lax.rem(me + k, ranks)})
    pl.semaphore_wait(barrier, ranks + 1)

    def push(src, dst, sems, i, where):
        copy = pltpu.make_async_remote_copy(
            src_ref=src,
            dst_ref=dst,
            send_sem=sems.at[0, i],
            recv_sem=sems.at[1, i],
            device_id=where,
        )
        copy.start()
        return copy

    pending = []

    tile_copies, ints_copies = [None], [None]
    ints_in[0] = ints_ref[me]
    for k in range(1, ranks):
        dst = lax.rem(me + k, ranks)
        slot = jnp.int32(0)
        for s in range(balanced):
            v = from_ref[dst * balanced + s]
            slot = jnp.where(v // hold == me, v % hold, slot)
        tile_out[k] = tiles_ref[slot]
        ints_copies.append(push(ints_ref.at[dst], ints_in.at[k], ints_sem, k, {"dp": dst}))
        tile_copies.append(push(tile_out.at[k], tile_in.at[k], tile_sem, k, {"dp": dst}))

    cols = patch_ref.shape[0]
    patch[0] = patch_ref[...]
    p_sib = push(patch_ref, patch.at[1], patch_sem, 0, {"tensor": sib})
    p_far = push(patch_ref, patch.at[2], patch_sem, 1, {"tensor": far})
    for k in range(1, ranks):
        ints_copies[k].wait_recv()
        tile_copies[k].wait_recv()
    p_far.wait_recv()
    p_fwd = push(patch.at[2], patch.at[3], patch_sem, 2, {"tensor": sib})

    positions = []
    lane = lax.broadcasted_iota(jnp.int32, (8, 128), 1)
    row = lax.broadcasted_iota(jnp.int32, (8, 128), 0)
    for s in range(balanced):
        v = from_ref[me * balanced + s]
        src = v // hold
        slot = v % hold
        behind = lax.rem(me - src + ranks, ranks)
        mine = (src == me).astype(F32)
        own = tiles_ref[slot].astype(F32)
        came = tile_in[behind].astype(F32)
        pix[0, s] = jnp.where(mine > 0.5, own, came).astype(BF16)
        found = jnp.where((row == 1) & (lane == slot), ints_in[behind], 0).astype(F32)
        place = jnp.sum(jnp.sum(found, axis=1, keepdims=True), axis=0, keepdims=True)
        line = jnp.zeros((1, dim), F32)
        for m in range(table_ref.shape[0]):
            line = line + jnp.where(place == float(m), table_ref[m : m + 1, :], 0.0)
        positions.append(line)
    x_sib = push(pix.at[0], pix.at[1], pix_sem, 0, {"tensor": sib})
    x_far = push(pix.at[0], pix.at[2], pix_sem, 1, {"tensor": far})

    slots_here = out_ref.shape[0]
    want = lax.broadcasted_iota(jnp.int32, (slots_here, 128), 0)
    lanes = lax.broadcasted_iota(jnp.int32, (slots_here, 128), 1)
    index = jnp.zeros((slots_here, 128), jnp.int32)
    for k in range(ranks):
        hit = (want == ints_in[k, 0:1, :]) & (lanes < cap)
        index = index + jnp.where(hit, k * cap + lanes + 1, 0)
    index = jnp.sum(index, axis=1, keepdims=True) - 1
    source_v[...] = jnp.broadcast_to(index, (slots_here, 128))
    to_scalar = pltpu.make_async_copy(source_v, source_s, s_sem.at[0])
    to_scalar.start()

    x_far.wait_recv()
    x_fwd = push(pix.at[2], pix.at[3], pix_sem, 2, {"tensor": sib})
    p_sib.wait_recv()
    p_fwd.wait_recv()
    x_sib.wait_recv()
    x_fwd.wait_recv()
    pending += [p_sib, p_far, p_fwd, x_sib, x_far, x_fwd]
    pending += tile_copies[1:] + ints_copies[1:]

    which = (t, sib, far, far_sib)

    full = jnp.concatenate
    for s in range(balanced):
        base = positions[s]
        for i in range(4):
            parts = []
            for j in range(4):
                rel = jnp.int32(0)
                for m in range(1, 4):
                    rel = jnp.where(which[m] == j, m, rel)
                parts.append(dot_t(pix[i, s], patch[rel]).astype(BF16).astype(F32))
            x = full(parts, axis=1) + base
            at = pl.multiple_of(which[i] * toks, toks)
            n1[s, pl.ds(at, toks), :] = normalise(x, g1_ref[...], b1_ref[...])

            @pl.when(core == s)
            def _():
                state[pl.ds(at, toks), :] = x

    for i in range(3):
        loads[i].wait()
    for b in range(2):
        act = n1[b]
        q_s[b] = dot(act, wq[...]).astype(BF16)
        k_s[b] = dot(act, wk[...]).astype(BF16)
        v_s[b] = dot(act, wv[...]).astype(BF16)

    head_lane = lax.broadcasted_iota(jnp.int32, (1, local_cols), 1)
    masks = [
        ((head_lane >= h * HEAD_DIM) & (head_lane < (h + 1) * HEAD_DIM)).astype(F32)
        for h in range(heads)
    ]

    def attend(b):
        q = q_s[b]
        keys = k_s[b]
        vals = v_s[b]
        total = jnp.zeros((length, local_cols), F32)
        for h in range(heads):
            qh = q * masks[h].astype(BF16)
            scores = dot_t(qh, keys) * HEAD_DIM ** (-0.5)
            top = jnp.max(scores, axis=-1, keepdims=True)
            e = jnp.exp(scores - top)
            p = (e / jnp.sum(e, axis=-1, keepdims=True)).astype(BF16)
            total = total + dot(p, vals) * masks[h]
        ctx[b] = total.astype(BF16)

    step = wide(dim)

    def merge(layer, source, weight, gain, bias, extra, normed):
        left = source[other]

        @pl.loop(0, dim // step)
        def _(j):
            at = pl.ds(pl.multiple_of(j * step, step), step)
            sib_out[layer, :, at] = dot(left, weight[:, at]).astype(BF16)

        first = []
        for r in range(CHUNKS):
            at = pl.ds(r * rows, rows)
            first.append(
                push(
                    sib_out.at[layer, at],
                    sib_in.at[layer, at],
                    sib_sem,
                    layer * CHUNKS + r,
                    {"tensor": sib},
                )
            )
        return first

    def merge_rest(layer, first, source, weight, gain, bias, extra, normed):
        right = source[core]

        @pl.loop(0, dim // step)
        def _(j):
            at = pl.ds(pl.multiple_of(j * step, step), step)
            acc[:, at] = dot(right, weight[:, at])

        second, third = [], []
        for r in range(CHUNKS):
            at = pl.ds(r * rows, rows)
            first[r].wait_recv()
            both = acc[at, :] + sib_in[layer, at, :].astype(F32)
            acc[at, :] = both
            x_out[layer, at, :] = both.astype(BF16)
            second.append(
                push(
                    x_out.at[layer, at],
                    x_in.at[layer, at],
                    x_sem,
                    layer * CHUNKS + r,
                    {"tensor": far},
                )
            )
        for r in range(CHUNKS):
            at = pl.ds(r * rows, rows)
            second[r].wait_recv()
            x = state[at, :] + (acc[at, :] + x_in[layer, at, :].astype(F32)) + extra
            state[at, :] = x
            normed[core, at, :] = normalise(x, gain[...], bias[...])
            third.append(
                push(
                    normed.at[core, at],
                    normed.at[core, at],
                    n_sem,
                    layer * CHUNKS + r,
                    {"tensor": sib},
                )
            )
        pending.extend(first + second + third)
        return third

    attend(other)
    loads[3].wait()
    args = (ctx, wo, g2_ref, b2_ref, 0.0, n2)
    first = merge(0, *args)
    attend(core)
    third = merge_rest(0, first, *args)

    loads[4].wait()
    loads[5].wait()
    ff = w1.shape[1]
    ff_step = wide(ff)

    def up(b):
        act = n2[b]

        @pl.loop(0, ff // ff_step)
        def _(j):
            at = pl.ds(pl.multiple_of(j * ff_step, ff_step), ff_step)
            inner = dot(act, w1[:, at]) + fb1_ref[:, at]
            gelu = inner * (1.0 + lax.erf(inner * (0.5**0.5))) * 0.5
            hid[b, :, at] = gelu.astype(BF16)

    up(core)
    for copy in third:
        copy.wait_recv()
    up(other)
    args = (hid, w2, g3_ref, b3_ref, fb2_ref[...], n3)
    first = merge(1, *args)
    third = merge_rest(1, first, *args)

    loads[6].wait()
    half = wkv.shape[1] // 2

    def pages(b):
        both = dot(n3[b], wkv[...])
        parts = []
        for h in range(half // KV_DIM):
            key = both[:, h * KV_DIM : (h + 1) * KV_DIM]
            size = jnp.mean(key * key, axis=-1, keepdims=True)
            parts.append(key * lax.rsqrt(size + 1e-05) * kg_ref[...])
        parts.append(both[:, half:])
        joined = full(parts, axis=1)
        per = length // PAGE
        kvp[pl.ds(b * per, per)] = joined.reshape(per, PAGE, 2 * half).astype(BF16)

    pages(core)
    for copy in third:
        copy.wait_recv()
    pages(other)

    to_scalar.wait()
    page_copies = []
    for k in list(range(1, ranks)) + [0]:
        dst = lax.rem(me + k, ranks)
        for j in range(cap):
            page = kvp[order_ref[dst * cap + j]]
            if k:
                page_out[k, j] = page
            else:
                page_in[0, j] = page
        if k:
            page_copies.append(push(page_out.at[k], page_in.at[k], page_sem, k, {"dp": dst}))
    for copy in page_copies:
        copy.wait_recv()
    pending.extend(page_copies)

    @pl.loop(0, slots_here)
    def _(m):
        at = source_s[m, 0]
        safe = jnp.clip(at, 0, ranks * cap - 1)
        page = page_in[safe // cap, safe % cap].astype(F32)
        out_ref[m] = jnp.where(at >= 0, page, 0.0).astype(BF16)

    for copy in pending:
        copy.wait_send()


def on_device(
    tiles,
    tile_index,
    tile_from,
    patch_weight,
    tile_table,
    ln1_gain,
    ln1_bias,
    qkv_weight,
    out_weight,
    ln2_gain,
    ln2_bias,
    fc1_weight,
    fc1_bias,
    fc2_weight,
    fc2_bias,
    ln3_gain,
    ln3_bias,
    kv_weight,
    knorm_gain,
    page_owner,
    page_slot,
):
    ranks = lax.axis_size("dp")
    hold, toks, patch = tiles.shape
    balanced = tile_from.shape[0] // ranks
    shards = lax.axis_size("tensor")
    length = toks * shards
    dim = out_weight.shape[1]
    page_count = page_owner.shape[0]
    cap = max(2, 2 * ((page_count + ranks - 1) // ranks))
    cache_slots = 2 * page_count

    numbers = jnp.arange(page_count, dtype=jnp.int32)
    earlier = (page_owner[:, None] == page_owner[None, :]) & (numbers[None, :] < numbers[:, None])
    target = page_owner * cap + jnp.sum(earlier.astype(jnp.int32), axis=1)
    places = jnp.arange(ranks * cap, dtype=jnp.int32)
    routed = target[None, :] == places[:, None]
    order = jnp.sum(jnp.where(routed, numbers[None, :], 0), axis=1)
    going = jnp.sum(jnp.where(routed, page_slot[None, :] + 1, 0), axis=1) - 1
    ints = jnp.concatenate(
        [
            jnp.pad(going.reshape(ranks, 1, cap), ((0, 0), (0, 0), (0, 128 - cap)), constant_values=-1),
            jnp.broadcast_to(jnp.pad(tile_index, (0, 128 - hold))[None, None, :], (ranks, 1, 128)),
            jnp.zeros((ranks, 6, 128), jnp.int32),
        ],
        axis=1,
    )
    padded = -(-patch // 128) * 128
    tiles = jnp.pad(tiles, ((0, 0), (0, 0), (0, padded - patch)))
    patch_t = jnp.pad(patch_weight, ((0, padded - patch), (0, 0))).T
    local = qkv_weight.shape[2]
    ff = fc1_weight.shape[1]
    kv_cols = 2 * kv_weight.shape[2]
    wkv = kv_weight.reshape(dim, kv_cols)
    vmem = pl.BlockSpec(memory_space=pltpu.VMEM)
    smem = pl.BlockSpec(memory_space=pltpu.SMEM)
    anywhere = pl.BlockSpec(memory_space=pl.ANY)

    def sems(count):
        return pltpu.SemaphoreType.DMA((2, count))

    pairs = 2 * CHUNKS
    kept = (2, length, dim)
    cache = pl.pallas_call(
        functools.partial(kernel, ranks, cap),
        out_shape=jax.ShapeDtypeStruct((cache_slots, PAGE, kv_cols), BF16),
        in_specs=[smem] * 2 + [vmem] * 13 + [anywhere] * 7,
        out_specs=vmem,
        scratch_shapes=[
            pltpu.VMEM((dim, local), BF16),
            pltpu.VMEM((dim, local), BF16),
            pltpu.VMEM((dim, local), BF16),
            pltpu.VMEM((local, dim), BF16),
            pltpu.VMEM((dim, ff), BF16),
            pltpu.VMEM((ff, dim), BF16),
            pltpu.VMEM((dim, kv_cols), BF16),
            pltpu.VMEM((shards,) + patch_t.shape, BF16),
            pltpu.VMEM((ranks, 8, 128), jnp.int32),
            pltpu.VMEM((ranks, toks, padded), BF16),
            pltpu.VMEM((ranks, toks, padded), BF16),
            pltpu.VMEM((shards, balanced, toks, padded), BF16),
            pltpu.VMEM((length, dim), F32),
            pltpu.VMEM(kept, BF16),
            pltpu.VMEM(kept, BF16),
            pltpu.VMEM(kept, BF16),
            pltpu.VMEM((2, length, local), BF16),
            pltpu.VMEM((2, length, local), BF16),
            pltpu.VMEM((2, length, local), BF16),
            pltpu.VMEM((2, length, local), BF16),
            pltpu.VMEM((2, length, ff), BF16),
            pltpu.VMEM((length, dim), F32),
            pltpu.VMEM(kept, BF16),
            pltpu.VMEM(kept, BF16),
            pltpu.VMEM(kept, BF16),
            pltpu.VMEM(kept, BF16),
            pltpu.VMEM((page_count, PAGE, kv_cols), BF16),
            pltpu.VMEM((ranks, cap, PAGE, kv_cols), BF16),
            pltpu.VMEM((ranks, cap, PAGE, kv_cols), BF16),
            pltpu.VMEM((cache_slots, 128), jnp.int32),
            pltpu.SMEM((cache_slots, 128), jnp.int32),
            pltpu.SemaphoreType.DMA((7,)),
            sems(ranks),
            sems(ranks),
            sems(ranks),
            sems(3),
            sems(3),
            sems(pairs),
            sems(pairs),
            sems(pairs),
            pltpu.SemaphoreType.DMA((1,)),
        ],
        compiler_params=pltpu.CompilerParams(
            collective_id=0, has_side_effects=True, vmem_limit_bytes=56 * 1024 * 1024
        ),
        name="encoder",
    )(
        tile_from,
        order,
        ints,
        tiles,
        patch_t,
        tile_table,
        ln1_gain[None],
        ln1_bias[None],
        ln2_gain[None],
        ln2_bias[None],
        ln3_gain[None],
        ln3_bias[None],
        fc1_bias[None],
        fc2_bias[None],
        knorm_gain[None],
        qkv_weight[:, 0],
        qkv_weight[:, 1],
        qkv_weight[:, 2],
        out_weight,
        fc1_weight,
        fc2_weight,
        wkv,
    )
    return cache.reshape(cache_slots, PAGE, 2, kv_cols // 2)


def solution(mesh):
    return jax.shard_map(
        on_device,
        mesh=mesh,
        in_specs=(
            P(("groups", "dp"), "tensor", None),
            P(("groups", "dp")),
            P("groups"),
            P(None, "tensor"),
            P(),
            P(),
            P(),
            P(None, None, "tensor"),
            P("tensor", None),
            P(),
            P(),
            P(None, "tensor"),
            P("tensor"),
            P("tensor", None),
            P(),
            P(),
            P(),
            P(None, None, "tensor"),
            P(),
            P(("groups", "dp")),
            P(("groups", "dp")),
        ),
        out_specs=P(("groups", "dp"), None, None, "tensor"),
        check_vma=False,
    )
```

time: 263 us -> 129 us (0.49)
  the two profiles are of different devices: /device:TPU:0 before, /device:TPU:15 now
where the time goes in v1:
time: 129 us; the launch traced here: 128 us
  Pallas kernels  103 us (80%)
  local copies, waits for them, and re-layouts  22.5 us (17%)
  other arithmetic  2.91 us (2%)
    pallas_call x1, Pallas kernels, on_device(): pl.pallas_call(functools.partial(kernel, ranks, cap), out_shape=jax.Shape...  103 us
    unnamed x8, local copies, waits for them, and re-layouts  5.24 us

profile of v1, /device:TPU:15, one launch (start us, length us, event | category | flops | bytes accessed | tf_op | source)
XLA Modules:
  0.0 128.0 jit_solution(5314183343282800283)
XLA Ops:
  0.0 0.8 pad.17
  0.8 0.9 convert_reduce_fusion
  1.7 0.1 pad.22.clone
  1.8 0.7 multiply_add_fusion
  2.4 0.7 select_reduce_fusion
  3.1 0.1 sub.7
  3.2 1.4 %broadcast_in_dim.67.g1_ref = f32[1,1280]{1,0:T(1,128)} reshape(f32[1280]{0:T(1024)} %param.26) | data formatting | bytes 10240 | tf_op jit(solution)/shard_map/broadcast_in_dim | solution.py:531
  4.6 1.3 %broadcast_in_dim.68.b1_ref = f32[1,1280]{1,0:T(1,128)} reshape(f32[1280]{0:T(1024)} %param.27) | data formatting | bytes 10240 | tf_op jit(solution)/shard_map/broadcast_in_dim | solution.py:532
  5.9 1.3 %broadcast_in_dim.69.g2_ref = f32[1,1280]{1,0:T(1,128)} reshape(f32[1280]{0:T(1024)} %param.30) | data formatting | bytes 10240 | tf_op jit(solution)/shard_map/broadcast_in_dim | solution.py:533
  7.2 1.3 %broadcast_in_dim.70.b2_ref = f32[1,1280]{1,0:T(1,128)} reshape(f32[1280]{0:T(1024)} %param.31) | data formatting | bytes 10240 | tf_op jit(solution)/shard_map/broadcast_in_dim | solution.py:534
  8.5 1.3 %broadcast_in_dim.73.fb1_ref = f32[1,1280]{1,0:T(1,128)} reshape(f32[1280]{0:T(1024)} %param.33) | data formatting | bytes 10240 | tf_op jit(solution)/shard_map/broadcast_in_dim | solution.py:537
  9.8 1.3 %broadcast_in_dim.74.fb2_ref = f32[1,1280]{1,0:T(1,128)} reshape(f32[1280]{0:T(1024)} %param.35) | data formatting | bytes 10240 | tf_op jit(solution)/shard_map/broadcast_in_dim | solution.py:538
  11.1 1.3 %broadcast_in_dim.71.g3_ref = f32[1,1280]{1,0:T(1,128)} reshape(f32[1280]{0:T(1024)} %param.36) | data formatting | bytes 10240 | tf_op jit(solution)/shard_map/broadcast_in_dim | solution.py:535
  12.4 1.3 %broadcast_in_dim.72.b3_ref = f32[1,1280]{1,0:T(1,128)} reshape(f32[1280]{0:T(1024)} %param.37) | data formatting | bytes 10240 | tf_op jit(solution)/shard_map/broadcast_in_dim | solution.py:536
  13.7 0.7 fusion.ints_ref
  14.3 1.7 %pad.18.tiles_ref = bf16[4,64,640]{2,1,0:T(8,128)(2,1)} pad(bf16[4,64,588]{2,1,0:T(8,128)(2,1)} %param.21, bf16[]{:T(256)} %constant.12.clone.1), padding=0_0x0_0x0_52 | pad | bytes 628738 | tf_op jit(solution)/shard_map/jit(_pad)/pad | solution.py:457
  16.1 1.8 %pad_bitcast_fusion.patch_ref = bf16[320,640]{1,0:T(8,128)(2,1)} fusion(bf16[588,320]{0,1:T(8,128)(2,1)} %param.24), kind=kLoop, calls=%fused_computation | loop fusion | bytes 785920 | tf_op jit(solution)/shard_map/transpose | solution.py:458
  17.9 1.3 %copy.33 = bf16[160,8,2,256]{3,1,2,0:T(8,128)(2,1)} copy(bf16[160,8,2,256]{3,2,1,0:T(2,128)(2,1)S(1)} %bitcast.13) | data formatting | bytes 2621440
  19.2 0.2 fusion.2
  19.4 1.3 %copy.32 = bf16[1280,1,320]{2,0,1:T(8,128)(2,1)} copy(bf16[1280,1,320]{0,2,1:T(8,128)(2,1)S(1)} %get-tuple-element.7) | data formatting | bytes 1638400
  20.7 1.3 %copy.31 = bf16[1280,1,320]{2,0,1:T(8,128)(2,1)} copy(bf16[1280,1,320]{0,2,1:T(8,128)(2,1)S(1)} %get-tuple-element.8) | data formatting | bytes 1638400
  22.0 1.3 %copy.30 = bf16[1280,1,320]{2,0,1:T(8,128)(2,1)} copy(bf16[1280,1,320]{0,2,1:T(8,128)(2,1)S(1)} %get-tuple-element.9) | data formatting | bytes 1638400
  23.3 102.6 %encoder.1 = bf16[64,16,512]{2,1,0:T(8,128)(2,1)} custom-call(s32[8]{0:T(128)} %from_ref.1, s32[64]{0:T(128)} %get-tuple-element.6.order_ref, s32[4,8,128]{2,1,0:T(8,128)} %fusion.ints_ref, bf16[4,64,640]{2,1,0:T(8,128)(2,1)} %pad.18.tiles_ref, bf16[320,640]{1,0:T(8,128)(2,1)} %pad_bitcast_fusion.patch_ref, f32[4,1280]{1,0:T(4,128)} %table_ref.1, ...), custom_call_target="tpu_custom_call" | custom-call | tf_op jit(solution)/shard_map/encoder/pallas_call | solution.py:472
  125.9 2.1 %reshape.28 = bf16[64,16,2,256]{3,2,1,0:T(2,128)(2,1)} reshape(bf16[64,16,512]{2,1,0:T(8,128)(2,1)} %encoder.1) | data formatting | bytes 2097152 | tf_op jit(solution)/shard_map/reshape | solution.py:548
  (7 shorter events, 0.0 us)
Async XLA Ops:
  0.0 17.9 %copy-start.1 = (bf16[1280,2,256]{2,1,0:T(2,128)(2,1)S(1)}, bf16[1280,2,256]{2,1,0:T(2,128)(2,1)}, u32[]{:S(2)}) copy-start(bf16[1280,2,256]{2,1,0:T(2,128)(2,1)} %param.38) | copy-start | bytes 3932164
  3.2 16.0 %copy-start = (bf16[1280,3,320]{0,2,1:T(8,128)(2,1)S(1)}, bf16[1280,3,320]{0,2,1:T(8,128)(2,1)}, u32[]{:S(2)}) copy-start(bf16[1280,3,320]{0,2,1:T(8,128)(2,1)} %param.28) | copy-start | bytes 7372804

commit v2 on v1

v2 whole, which is shorter than its diff:
```python
import functools

import jax
import jax.numpy as jnp
from jax import lax
from jax.experimental import pallas as pl
from jax.experimental.pallas import tpu as pltpu
from jax.sharding import PartitionSpec as P

HEAD_DIM = 80
KV_DIM = 128
PAGE = 16
CHUNKS = 4
F32 = jnp.float32
BF16 = jnp.bfloat16


def normalise(x, gain, bias):
    mean = jnp.mean(x, axis=-1, keepdims=True)
    centred = x - mean
    spread = jnp.mean(centred * centred, axis=-1, keepdims=True)
    return (centred * lax.rsqrt(spread + 1e-05) * gain + bias).astype(BF16)


def dot(a, b):
    return jnp.dot(a, b, preferred_element_type=F32)


def dot_t(a, b):
    return lax.dot_general(a, b, (((1,), (1,)), ((), ())), preferred_element_type=F32)


def wide(total):
    return 256 if total % 256 == 0 else total


def kernel(
    ranks,
    cap,
    from_ref,
    position_ref,
    owner_ref,
    slot_ref,
    tiles_ref,
    patch_ref,
    table_ref,
    g1_in,
    b1_in,
    g2_in,
    b2_in,
    g3_in,
    b3_in,
    fb2_in,
    fb1_in,
    kg_ref,
    wqkv_hbm,
    wo_hbm,
    w1_hbm,
    w2_hbm,
    wkv_hbm,
    out_ref,
    wqkv,
    wo,
    w1,
    w2,
    wkv,
    patch,
    ints_out,
    ints_in,
    order_v,
    order_s,
    vec,
    fb1_ref,
    tile_out,
    tile_in,
    pix,
    state,
    n1,
    n2,
    n3,
    q_s,
    k_s,
    v_s,
    ctx,
    hid,
    acc,
    sib_out,
    sib_in,
    x_out,
    x_in,
    kvp,
    page_out,
    page_in,
    source_v,
    source_s,
    wsem,
    ints_sem,
    tile_sem,
    page_sem,
    patch_sem,
    pix_sem,
    sib_sem,
    x_sem,
    n_sem,
    s_sem,
):
    me = lax.axis_index("dp")
    t = lax.axis_index("tensor")
    core = lax.rem(t, 2)
    other = 1 - core
    sib = t + 1 - 2 * core
    far = lax.rem(t + 2, 4)
    far_sib = lax.rem(sib + 2, 4)
    hold, toks, width = tiles_ref.shape
    balanced = from_ref.shape[0] // ranks
    length = state.shape[0]
    dim = state.shape[1]
    rows = length // CHUNKS
    local_cols = wqkv.shape[1]
    heads = local_cols // HEAD_DIM

    weights = [
        (wqkv_hbm, wqkv),
        (wo_hbm, wo),
        (w1_hbm, w1),
        (w2_hbm, w2),
        (wkv_hbm, wkv),
    ]
    loads = [pltpu.make_async_copy(a, b, wsem.at[i]) for i, (a, b) in enumerate(weights)]
    for load in loads:
        load.start()

    barrier = pltpu.get_barrier_semaphore()
    for peer in (sib, far):
        pl.semaphore_signal(barrier, inc=1, device_id={"tensor": peer})
    for k in range(1, ranks):
        pl.semaphore_signal(barrier, inc=1, device_id={"dp": lax.rem(me + k, ranks)})
    pl.semaphore_wait(barrier, ranks + 1)

    def push(src, dst, sems, i, where):
        copy = pltpu.make_async_remote_copy(
            src_ref=src,
            dst_ref=dst,
            send_sem=sems.at[0, i],
            recv_sem=sems.at[1, i],
            device_id=where,
        )
        copy.start()
        return copy

    pending = []

    width_r = order_v.shape[0]
    row = lax.broadcasted_iota(jnp.int32, (width_r, 128), 0)
    lane = lax.broadcasted_iota(jnp.int32, (width_r, 128), 1)

    def assign(p, carry):
        count, order, going = carry
        owned = row == owner_ref[p]
        hit = owned & (lane == count)
        order = jnp.where(hit, p, order)
        going = jnp.where(hit, slot_ref[p], going)
        return count + jnp.where(owned, 1, 0), order, going

    zero = jnp.zeros((width_r, 128), jnp.int32)
    _, order, going = lax.fori_loop(0, owner_ref.shape[0], assign, (zero, zero, zero - 1))
    order_v[...] = order
    to_scalar = [pltpu.make_async_copy(order_v, order_s, s_sem.at[1])]
    to_scalar[0].start()
    ints_out[0:width_r, :] = going
    spots = jnp.zeros((8, 128), jnp.int32)
    lane8 = lax.broadcasted_iota(jnp.int32, (8, 128), 1)
    for i in range(hold):
        spots = jnp.where(lane8 == i, position_ref[i], spots)
    ints_out[width_r : width_r + 8, :] = spots
    ints_in[0] = ints_out[...]

    tile_copies, ints_copies = [None], [None]
    for k in range(1, ranks):
        dst = lax.rem(me + k, ranks)
        slot = jnp.int32(0)
        for s in range(balanced):
            v = from_ref[dst * balanced + s]
            slot = jnp.where(v // hold == me, v % hold, slot)
        tile_out[k] = tiles_ref[slot]
        ints_copies.append(push(ints_out, ints_in.at[k], ints_sem, k, {"dp": dst}))
        tile_copies.append(push(tile_out.at[k], tile_in.at[k], tile_sem, k, {"dp": dst}))

    patch[t] = patch_ref[...]
    p_sib = push(patch_ref, patch.at[t], patch_sem, 0, {"tensor": sib})
    p_far = push(patch_ref, patch.at[t], patch_sem, 1, {"tensor": far})
    for i, ref in enumerate((g1_in, b1_in, g2_in, b2_in, g3_in, b3_in, fb2_in)):
        vec[i : i + 1, :] = ref[...].reshape(1, dim)
    fb1_ref[...] = fb1_in[...].reshape(fb1_ref.shape)
    g1, b1, g2, b2, g3, b3, fb2 = [vec.at[i : i + 1] for i in range(7)]
    for k in range(1, ranks):
        ints_copies[k].wait_recv()
        tile_copies[k].wait_recv()

    positions = []
    row8 = lax.broadcasted_iota(jnp.int32, (8, 128), 0)
    for s in range(balanced):
        v = from_ref[me * balanced + s]
        src = v // hold
        slot = v % hold
        behind = lax.rem(me - src + ranks, ranks)
        mine = (src == me).astype(F32)
        own = tiles_ref[slot].astype(F32)
        came = tile_in[behind].astype(F32)
        pix[t, s * toks : (s + 1) * toks, :] = jnp.where(mine > 0.5, own, came).astype(BF16)
        found = jnp.where(
            (row8 == 0) & (lane8 == slot), ints_in[behind, width_r : width_r + 8, :], 0
        ).astype(F32)
        place = jnp.sum(jnp.sum(found, axis=1, keepdims=True), axis=0, keepdims=True)
        line = jnp.zeros((1, dim), F32)
        for m in range(table_ref.shape[0]):
            line = line + jnp.where(place == float(m), table_ref[m : m + 1, :], 0.0)
        positions.append(line)
    x_sib = push(pix.at[t], pix.at[t], pix_sem, 0, {"tensor": sib})
    x_far = push(pix.at[t], pix.at[t], pix_sem, 1, {"tensor": far})
    p_far.wait_recv()
    p_fwd = push(patch.at[far], patch.at[far], patch_sem, 2, {"tensor": sib})

    slots_here = out_ref.shape[0]
    want = lax.broadcasted_iota(jnp.int32, (slots_here, 128), 0)
    lanes = lax.broadcasted_iota(jnp.int32, (slots_here, 128), 1)
    index = jnp.zeros((slots_here, 128), jnp.int32)
    for k in range(ranks):
        hit = (want == ints_in[k, pl.ds(me, 1), :]) & (lanes < cap)
        index = index + jnp.where(hit, k * cap + lanes + 1, 0)
    index = jnp.sum(index, axis=1, keepdims=True) - 1
    source_v[...] = jnp.broadcast_to(index, (slots_here, 128))
    to_scalar.append(pltpu.make_async_copy(source_v, source_s, s_sem.at[0]))
    to_scalar[1].start()

    full = jnp.concatenate
    p_sib.wait_recv()
    p_fwd.wait_recv()

    def embed(i):
        x = dot_t(pix[i], patch[...].reshape(dim, width)).astype(BF16).astype(F32)
        at = pl.ds(pl.multiple_of(i * toks, toks), toks)
        for s in range(balanced):
            y = x[s * toks : (s + 1) * toks] + positions[s]
            n1[s, at, :] = normalise(y, g1[...], b1[...])

            @pl.when(core == s)
            def _():
                state[at, :] = y

    embed(t)
    x_far.wait_recv()
    x_fwd = push(pix.at[far], pix.at[far], pix_sem, 2, {"tensor": sib})
    x_sib.wait_recv()
    embed(sib)
    embed(far)
    x_fwd.wait_recv()
    embed(far_sib)
    pending += [p_sib, p_far, p_fwd, x_sib, x_far, x_fwd]
    pending += tile_copies[1:] + ints_copies[1:]

    loads[0].wait()
    for b in range(2):
        act = n1[b]
        q_s[b] = dot_t(act, wqkv[0]).astype(BF16)
        k_s[b] = dot_t(act, wqkv[1]).astype(BF16)
        v_s[b] = dot_t(act, wqkv[2]).astype(BF16)

    head_lane = lax.broadcasted_iota(jnp.int32, (1, local_cols), 1)
    masks = [
        ((head_lane >= h * HEAD_DIM) & (head_lane < (h + 1) * HEAD_DIM)).astype(F32)
        for h in range(heads)
    ]

    def attend(b):
        q = q_s[b]
        keys = k_s[b]
        vals = v_s[b]
        total = jnp.zeros((length, local_cols), F32)
        for h in range(heads):
            qh = q * masks[h].astype(BF16)
            scores = dot_t(qh, keys) * HEAD_DIM ** (-0.5)
            top = jnp.max(scores, axis=-1, keepdims=True)
            e = jnp.exp(scores - top)
            p = (e / jnp.sum(e, axis=-1, keepdims=True)).astype(BF16)
            total = total + dot(p, vals) * masks[h]
        ctx[b] = total.astype(BF16)

    step = wide(dim)

    def project(layer, source, weight, lo, hi):
        span = pl.ds(lo * rows, (hi - lo) * rows)
        left = source[other, span, :]

        @pl.loop(0, dim // step)
        def _(j):
            at = pl.ds(pl.multiple_of(j * step, step), step)
            sib_out[layer, span, at] = dot(left, weight[:, at]).astype(BF16)

        copies = []
        for r in range(lo, hi):
            at = pl.ds(r * rows, rows)
            i = layer * CHUNKS + r
            copies.append(
                push(
                    sib_out.at[layer, at],
                    sib_in.at[layer, at],
                    sib_sem,
                    i,
                    {"tensor": sib},
                )
            )
        return copies

    def own(source, weight, lo, hi):
        span = pl.ds(lo * rows, (hi - lo) * rows)
        right = source[core, span, :]

        @pl.loop(0, dim // step)
        def _(j):
            at = pl.ds(pl.multiple_of(j * step, step), step)
            acc[span, at] = dot(right, weight[:, at])

    def cross(layer, near, lo, hi):
        copies = []
        for r in range(lo, hi):
            at = pl.ds(r * rows, rows)
            i = layer * CHUNKS + r
            near[r - lo].wait_recv()
            both = acc[at, :] + sib_in[layer, at, :].astype(F32)
            acc[at, :] = both
            x_out[layer, at, :] = both.astype(BF16)
            copies.append(
                push(x_out.at[layer, at], x_in.at[layer, at], x_sem, i, {"tensor": far})
            )
        pending.extend(near + copies)
        return copies

    def settle(layer, across, lo, hi, gain, bias, extra, normed):
        copies = []
        for r in range(lo, hi):
            at = pl.ds(r * rows, rows)
            i = layer * CHUNKS + r
            across[r].wait_recv()
            x = state[at, :] + (acc[at, :] + x_in[layer, at, :].astype(F32)) + extra
            state[at, :] = x
            normed[core, at, :] = normalise(x, gain[...], bias[...])
            copies.append(
                push(normed.at[core, at], normed.at[core, at], n_sem, i, {"tensor": sib})
            )
        pending.extend(copies)
        return copies

    attend(other)
    loads[1].wait()
    near = project(0, ctx, wo, 0, CHUNKS)
    attend(core)
    own(ctx, wo, 0, CHUNKS)
    across0 = cross(0, near, 0, CHUNKS)

    loads[2].wait()
    loads[3].wait()
    ff = w1.shape[1]
    ff_step = wide(ff)
    group = CHUNKS // 2

    def up(b, lo, hi):
        span = pl.ds(lo * rows, (hi - lo) * rows)
        act = n2[b, span, :]

        @pl.loop(0, ff // ff_step)
        def _(j):
            at = pl.ds(pl.multiple_of(j * ff_step, ff_step), ff_step)
            inner = dot(act, w1[:, at]) + fb1_ref[:, at]
            gelu = inner * (1.0 + lax.erf(inner * (0.5**0.5))) * 0.5
            hid[b, span, at] = gelu.astype(BF16)

    across1 = []
    for lo in range(0, CHUNKS, group):
        hi = lo + group
        came = settle(0, across0, lo, hi, g2, b2, 0.0, n2)
        up(core, lo, hi)
        for copy in came:
            copy.wait_recv()
        up(other, lo, hi)
        near = project(1, hid, w2, lo, hi)
        own(hid, w2, lo, hi)
        across1 += cross(1, near, lo, hi)

    loads[4].wait()
    half = wkv.shape[1] // 2

    def pages(b, lo, hi):
        count = (hi - lo) * rows
        both = dot(n3[b, pl.ds(lo * rows, count), :], wkv[...])
        parts = []
        for h in range(half // KV_DIM):
            key = both[:, h * KV_DIM : (h + 1) * KV_DIM]
            size = jnp.mean(key * key, axis=-1, keepdims=True)
            parts.append(key * lax.rsqrt(size + 1e-05) * kg_ref[...])
        parts.append(both[:, half:])
        joined = full(parts, axis=1)
        first = b * (length // PAGE) + lo * rows // PAGE
        kvp[pl.ds(first, count // PAGE)] = joined.reshape(count // PAGE, PAGE, 2 * half).astype(BF16)

    for lo in range(0, CHUNKS, group):
        hi = lo + group
        came = settle(1, across1, lo, hi, g3, b3, fb2[...], n3)
        pages(core, lo, hi)
        for copy in came:
            copy.wait_recv()
        pages(other, lo, hi)

    for copy in to_scalar:
        copy.wait()
    page_copies = []
    for k in list(range(1, ranks)) + [0]:
        dst = lax.rem(me + k, ranks)
        for j in range(cap):
            page = kvp[order_s[dst, j]]
            if k:
                page_out[k, j] = page
            else:
                page_in[0, j] = page
        if k:
            page_copies.append(push(page_out.at[k], page_in.at[k], page_sem, k, {"dp": dst}))
    for copy in page_copies:
        copy.wait_recv()
    pending.extend(page_copies)

    @pl.loop(0, slots_here)
    def _(m):
        at = source_s[m, 0]
        safe = jnp.clip(at, 0, ranks * cap - 1)
        page = page_in[safe // cap, safe % cap].astype(F32)
        out_ref[m] = jnp.where(at >= 0, page, 0.0).astype(BF16)

    for copy in pending:
        copy.wait_send()


def on_device(
    tiles,
    tile_index,
    tile_from,
    patch_weight,
    tile_table,
    ln1_gain,
    ln1_bias,
    qkv_weight,
    out_weight,
    ln2_gain,
    ln2_bias,
    fc1_weight,
    fc1_bias,
    fc2_weight,
    fc2_bias,
    ln3_gain,
    ln3_bias,
    kv_weight,
    knorm_gain,
    page_owner,
    page_slot,
):
    ranks = lax.axis_size("dp")
    hold, toks, patch = tiles.shape
    balanced = tile_from.shape[0] // ranks
    shards = lax.axis_size("tensor")
    length = toks * shards
    dim = out_weight.shape[1]
    page_count = page_owner.shape[0]
    cap = max(2, 2 * ((page_count + ranks - 1) // ranks))
    cache_slots = 2 * page_count
    owner_rows = -(-ranks // 8) * 8
    local = qkv_weight.shape[2]
    ff = fc1_weight.shape[1]
    kv_cols = 2 * kv_weight.shape[2]
    wkv = kv_weight.reshape(dim, kv_cols)
    vmem = pl.BlockSpec(memory_space=pltpu.VMEM)
    smem = pl.BlockSpec(memory_space=pltpu.SMEM)
    anywhere = pl.BlockSpec(memory_space=pl.ANY)

    def sems(count):
        return pltpu.SemaphoreType.DMA((2, count))

    pairs = 2 * CHUNKS
    kept = (2, length, dim)
    cache = pl.pallas_call(
        functools.partial(kernel, ranks, cap),
        out_shape=jax.ShapeDtypeStruct((cache_slots, PAGE, kv_cols), BF16),
        in_specs=[smem] * 4 + [vmem] * 12 + [anywhere] * 5,
        out_specs=vmem,
        scratch_shapes=[
            pltpu.VMEM((3, local, dim), BF16),
            pltpu.VMEM((local, dim), BF16),
            pltpu.VMEM((dim, ff), BF16),
            pltpu.VMEM((ff, dim), BF16),
            pltpu.VMEM((dim, kv_cols), BF16),
            pltpu.VMEM((shards, dim // shards, patch), BF16),
            pltpu.VMEM((owner_rows + 8, 128), jnp.int32),
            pltpu.VMEM((ranks, owner_rows + 8, 128), jnp.int32),
            pltpu.VMEM((owner_rows, 128), jnp.int32),
            pltpu.SMEM((owner_rows, 128), jnp.int32),
            pltpu.VMEM((8, dim), F32),
            pltpu.VMEM((1, ff), F32),
            pltpu.VMEM((ranks, toks, patch), BF16),
            pltpu.VMEM((ranks, toks, patch), BF16),
            pltpu.VMEM((shards, balanced * toks, patch), BF16),
            pltpu.VMEM((length, dim), F32),
            pltpu.VMEM(kept, BF16),
            pltpu.VMEM(kept, BF16),
            pltpu.VMEM(kept, BF16),
            pltpu.VMEM((2, length, local), BF16),
            pltpu.VMEM((2, length, local), BF16),
            pltpu.VMEM((2, length, local), BF16),
            pltpu.VMEM((2, length, local), BF16),
            pltpu.VMEM((2, length, ff), BF16),
            pltpu.VMEM((length, dim), F32),
            pltpu.VMEM(kept, BF16),
            pltpu.VMEM(kept, BF16),
            pltpu.VMEM(kept, BF16),
            pltpu.VMEM(kept, BF16),
            pltpu.VMEM((page_count, PAGE, kv_cols), BF16),
            pltpu.VMEM((ranks, cap, PAGE, kv_cols), BF16),
            pltpu.VMEM((ranks, cap, PAGE, kv_cols), BF16),
            pltpu.VMEM((cache_slots, 128), jnp.int32),
            pltpu.SMEM((cache_slots, 128), jnp.int32),
            pltpu.SemaphoreType.DMA((5,)),
            sems(ranks),
            sems(ranks),
            sems(ranks),
            sems(3),
            sems(3),
            sems(pairs),
            sems(pairs),
            sems(pairs),
            pltpu.SemaphoreType.DMA((2,)),
        ],
        compiler_params=pltpu.CompilerParams(
            collective_id=0, has_side_effects=True, vmem_limit_bytes=56 * 1024 * 1024
        ),
        name="encoder",
    )(
        tile_from,
        tile_index,
        page_owner,
        page_slot,
        tiles,
        patch_weight.T,
        tile_table,
        ln1_gain,
        ln1_bias,
        ln2_gain,
        ln2_bias,
        ln3_gain,
        ln3_bias,
        fc2_bias,
        fc1_bias,
        knorm_gain[None],
        qkv_weight.transpose(1, 2, 0),
        out_weight,
        fc1_weight,
        fc2_weight,
        wkv,
    )
    return cache.reshape(cache_slots, PAGE, 2, kv_cols // 2)


def solution(mesh):
    return jax.shard_map(
        on_device,
        mesh=mesh,
        in_specs=(
            P(("groups", "dp"), "tensor", None),
            P(("groups", "dp")),
            P("groups"),
            P(None, "tensor"),
            P(),
            P(),
            P(),
            P(None, None, "tensor"),
            P("tensor", None),
            P(),
            P(),
            P(None, "tensor"),
            P("tensor"),
            P("tensor", None),
            P(),
            P(),
            P(),
            P(None, None, "tensor"),
            P(),
            P(("groups", "dp")),
            P(("groups", "dp")),
        ),
        out_specs=P(("groups", "dp"), None, None, "tensor"),
        check_vma=False,
    )
```

time: 129 us -> 94.9 us (0.74)
  local copies, waits for them, and re-layouts: 22.5 us -> 4.79 us
  Pallas kernels: 103 us -> 88.9 us
  other arithmetic: 2.91 us -> 0 us
    pallas_call x1, Pallas kernels: 103 us -> 88.9 us  [on_device(): pl.pallas_call(functools.partial(kernel, ranks, cap), out_shape=jax.Shape...]
    broadcast_in_dim x10 -> x0, local copies, waits for them, and re-layouts: 10.5 us -> none  [the longest x1 1.44 us: on_device(): ln1_gain[None]]
    unnamed x8 -> x1, local copies, waits for them, and re-layouts: 5.24 us -> 2.65 us
    pad x2 -> x0, local copies, waits for them, and re-layouts: 2.51 us -> none  [the longest x1 1.75 us: on_device(): tiles = jnp.pad(tiles, ((0, 0), (0, 0), (0, padded - patch)))]
    transpose x1 -> x0, local copies, waits for them, and re-layouts: 1.79 us -> none  [on_device(): patch_t = jnp.pad(patch_weight, ((0, padded - patch), (0, 0))).T]
    reduce_sum x2 -> x0, other arithmetic: 1.56 us -> none  [the longest x1 0.91 us: on_device(): target = page_owner * cap + jnp.sum(earlier.astype(jnp.int32), axis=1)]
where the time goes in v2:
time: 94.9 us; the launch traced here: 93.7 us
  Pallas kernels  88.9 us (94%)
  local copies, waits for them, and re-layouts  4.79 us (5%)
    pallas_call x1, Pallas kernels, on_device(): pl.pallas_call(functools.partial(kernel, ranks, cap), out_shape=jax.Shape...  88.9 us
    unnamed x1, local copies, waits for them, and re-layouts  2.65 us
    reshape x1, local copies, waits for them, and re-layouts, on_device(): return cache.reshape(cache_slots, PAGE, 2, kv_cols // 2)  2.14 us

profile of v2, /device:TPU:15, one launch (start us, length us, event | category | flops | bytes accessed | tf_op | source)
XLA Modules:
  0.0 93.7 jit_solution(146319857811120757)
XLA Ops:
  0.0 2.6 %copy.22 = bf16[160,8,2,256]{3,1,2,0:T(8,128)(2,1)} copy(bf16[160,8,2,256]{3,2,1,0:T(2,128)(2,1)} %bitcast.7) | data formatting | bytes 2621440
  2.6 88.9 %encoder.1 = bf16[64,16,512]{2,1,0:T(8,128)(2,1)} custom-call(s32[8]{0:T(128)} %from_ref.1, s32[4]{0:T(128)} %position_ref.1, s32[32]{0:T(128)} %owner_ref.1, s32[32]{0:T(128)} %slot_ref.1, bf16[4,64,588]{2,1,0:T(8,128)(2,1)} %tiles_ref.1, bf16[320,588]{1,0:T(8,128)(2,1)} %bitcast.8, f32[4,1280]{1,0:T(4,128)} %table_ref.1, f32[1280]{0:T(1024)} %g1_in.1, ...), custom_call_target="tpu_custom_call" | custom-call | tf_op jit(solution)/shard_map/encoder/pallas_call | solution.py:488
  91.6 2.1 %reshape.7 = bf16[64,16,2,256]{3,2,1,0:T(2,128)(2,1)} reshape(bf16[64,16,512]{2,1,0:T(8,128)(2,1)} %encoder.1) | data formatting | bytes 2097152 | tf_op jit(solution)/shard_map/reshape | solution.py:566

commit v3 on v2

--- a/solution.py
+++ b/solution.py
@@ -63,10 +63,13 @@
     wo,
     w1,
     w2,
+    wkv_raw,
     wkv,
     patch,
     ints_out,
     ints_in,
+    spots_out,
+    spots_in,
     order_v,
     order_s,
     vec,
@@ -95,6 +98,7 @@
     source_s,
     wsem,
     ints_sem,
+    spot_sem,
     tile_sem,
     page_sem,
     patch_sem,
@@ -124,7 +128,7 @@
         (wo_hbm, wo),
         (w1_hbm, w1),
         (w2_hbm, w2),
-        (wkv_hbm, wkv),
+        (wkv_hbm, wkv_raw),
     ]
     loads = [pltpu.make_async_copy(a, b, wsem.at[i]) for i, (a, b) in enumerate(weights)]
     for load in loads:
@@ -150,32 +154,13 @@
 
     pending = []
 
-    width_r = order_v.shape[0]
-    row = lax.broadcasted_iota(jnp.int32, (width_r, 128), 0)
-    lane = lax.broadcasted_iota(jnp.int32, (width_r, 128), 1)
-
-    def assign(p, carry):
-        count, order, going = carry
-        owned = row == owner_ref[p]
-        hit = owned & (lane == count)
-        order = jnp.where(hit, p, order)
-        going = jnp.where(hit, slot_ref[p], going)
-        return count + jnp.where(owned, 1, 0), order, going
-
-    zero = jnp.zeros((width_r, 128), jnp.int32)
-    _, order, going = lax.fori_loop(0, owner_ref.shape[0], assign, (zero, zero, zero - 1))
-    order_v[...] = order
-    to_scalar = [pltpu.make_async_copy(order_v, order_s, s_sem.at[1])]
-    to_scalar[0].start()
-    ints_out[0:width_r, :] = going
+    lane8 = lax.broadcasted_iota(jnp.int32, (8, 128), 1)
     spots = jnp.zeros((8, 128), jnp.int32)
-    lane8 = lax.broadcasted_iota(jnp.int32, (8, 128), 1)
     for i in range(hold):
         spots = jnp.where(lane8 == i, position_ref[i], spots)
-    ints_out[width_r : width_r + 8, :] = spots
-    ints_in[0] = ints_out[...]
-
-    tile_copies, ints_copies = [None], [None]
+    spots_out[...] = spots
+    spots_in[0] = spots
+    tile_copies, spot_copies = [None], [None]
     for k in range(1, ranks):
         dst = lax.rem(me + k, ranks)
         slot = jnp.int32(0)
@@ -183,7 +168,7 @@
             v = from_ref[dst * balanced + s]
             slot = jnp.where(v // hold == me, v % hold, slot)
         tile_out[k] = tiles_ref[slot]
-        ints_copies.append(push(ints_out, ints_in.at[k], ints_sem, k, {"dp": dst}))
+        spot_copies.append(push(spots_out, spots_in.at[k], spot_sem, k, {"dp": dst}))
         tile_copies.append(push(tile_out.at[k], tile_in.at[k], tile_sem, k, {"dp": dst}))
 
     patch[t] = patch_ref[...]
@@ -194,7 +179,7 @@
     fb1_ref[...] = fb1_in[...].reshape(fb1_ref.shape)
     g1, b1, g2, b2, g3, b3, fb2 = [vec.at[i : i + 1] for i in range(7)]
     for k in range(1, ranks):
-        ints_copies[k].wait_recv()
+        spot_copies[k].wait_recv()
         tile_copies[k].wait_recv()
 
     positions = []
@@ -209,7 +194,7 @@
         came = tile_in[behind].astype(F32)
         pix[t, s * toks : (s + 1) * toks, :] = jnp.where(mine > 0.5, own, came).astype(BF16)
         found = jnp.where(
-            (row8 == 0) & (lane8 == slot), ints_in[behind, width_r : width_r + 8, :], 0
+            (row8 == 0) & (lane8 == slot), spots_in[behind], 0
         ).astype(F32)
         place = jnp.sum(jnp.sum(found, axis=1, keepdims=True), axis=0, keepdims=True)
         line = jnp.zeros((1, dim), F32)
@@ -221,50 +206,61 @@
     p_far.wait_recv()
     p_fwd = push(patch.at[far], patch.at[far], patch_sem, 2, {"tensor": sib})
 
-    slots_here = out_ref.shape[0]
-    want = lax.broadcasted_iota(jnp.int32, (slots_here, 128), 0)
-    lanes = lax.broadcasted_iota(jnp.int32, (slots_here, 128), 1)
-    index = jnp.zeros((slots_here, 128), jnp.int32)
-    for k in range(ranks):
-        hit = (want == ints_in[k, pl.ds(me, 1), :]) & (lanes < cap)
-        index = index + jnp.where(hit, k * cap + lanes + 1, 0)
-    index = jnp.sum(index, axis=1, keepdims=True) - 1
-    source_v[...] = jnp.broadcast_to(index, (slots_here, 128))
-    to_scalar.append(pltpu.make_async_copy(source_v, source_s, s_sem.at[0]))
-    to_scalar[1].start()
+    width_r = order_v.shape[0]
+    row = lax.broadcasted_iota(jnp.int32, (width_r, 128), 0)
+    lane = lax.broadcasted_iota(jnp.int32, (width_r, 128), 1)
+
+    def assign(p, carry):
+        count, order, going = carry
+        owned = row == owner_ref[p]
+        hit = owned & (lane == count)
+        order = jnp.where(hit, p, order)
+        going = jnp.where(hit, slot_ref[p], going)
+        return count + jnp.where(owned, 1, 0), order, going
+
+    zero = jnp.zeros((width_r, 128), jnp.int32)
+    _, order, going = lax.fori_loop(0, owner_ref.shape[0], assign, (zero, zero, zero - 1))
+    order_v[...] = order
+    to_scalar = [pltpu.make_async_copy(order_v, order_s, s_sem.at[1])]
+    to_scalar[0].start()
+    ints_out[...] = going
+    ints_in[0] = going
+    ints_copies = [None]
+    for k in range(1, ranks):
+        dst = lax.rem(me + k, ranks)
+        ints_copies.append(push(ints_out, ints_in.at[k], ints_sem, k, {"dp": dst}))
 
     full = jnp.concatenate
     p_sib.wait_recv()
     p_fwd.wait_recv()
 
-    def embed(i):
-        x = dot_t(pix[i], patch[...].reshape(dim, width)).astype(BF16).astype(F32)
-        at = pl.ds(pl.multiple_of(i * toks, toks), toks)
-        for s in range(balanced):
-            y = x[s * toks : (s + 1) * toks] + positions[s]
-            n1[s, at, :] = normalise(y, g1[...], b1[...])
-
-            @pl.when(core == s)
-            def _():
-                state[at, :] = y
-
-    embed(t)
+    def embed(first, second):
+        both = full([pix[first], pix[second]], axis=0)
+        x = dot_t(both, patch[...].reshape(dim, width)).astype(BF16).astype(F32)
+        for n, i in enumerate((first, second)):
+            at = pl.ds(pl.multiple_of(i * toks, toks), toks)
+            for s in range(balanced):
+                low = (n * balanced + s) * toks
+                y = x[low : low + toks] + positions[s]
+                n1[s, at, :] = normalise(y, g1[...], b1[...])
+
+                @pl.when(core == s)
+                def _():
+                    state[at, :] = y
+
+    x_sib.wait_recv()
+    embed(t, sib)
     x_far.wait_recv()
     x_fwd = push(pix.at[far], pix.at[far], pix_sem, 2, {"tensor": sib})
-    x_sib.wait_recv()
-    embed(sib)
-    embed(far)
     x_fwd.wait_recv()
-    embed(far_sib)
+    embed(far, far_sib)
     pending += [p_sib, p_far, p_fwd, x_sib, x_far, x_fwd]
-    pending += tile_copies[1:] + ints_copies[1:]
+    pending += tile_copies[1:] + spot_copies[1:] + ints_copies[1:]
 
     loads[0].wait()
-    for b in range(2):
-        act = n1[b]
-        q_s[b] = dot_t(act, wqkv[0]).astype(BF16)
-        k_s[b] = dot_t(act, wqkv[1]).astype(BF16)
-        v_s[b] = dot_t(act, wqkv[2]).astype(BF16)
+    act = n1[...].reshape(2 * length, dim)
+    for i, kept in enumerate((q_s, k_s, v_s)):
+        kept[...] = dot_t(act, wqkv[i]).astype(BF16).reshape(2, length, local_cols)
 
     head_lane = lax.broadcasted_iota(jnp.int32, (1, local_cols), 1)
     masks = [
@@ -272,30 +268,34 @@
         for h in range(heads)
     ]
 
-    def attend(b):
-        q = q_s[b]
+    def attend(b, lo, hi):
+        span = pl.ds(lo * rows, (hi - lo) * rows)
+        q = q_s[b, span, :]
         keys = k_s[b]
         vals = v_s[b]
-        total = jnp.zeros((length, local_cols), F32)
+        total = jnp.zeros(q.shape, F32)
         for h in range(heads):
             qh = q * masks[h].astype(BF16)
             scores = dot_t(qh, keys) * HEAD_DIM ** (-0.5)
             top = jnp.max(scores, axis=-1, keepdims=True)
             e = jnp.exp(scores - top)
-            p = (e / jnp.sum(e, axis=-1, keepdims=True)).astype(BF16)
+            p = (e * (1.0 / jnp.sum(e, axis=-1, keepdims=True))).astype(BF16)
             total = total + dot(p, vals) * masks[h]
-        ctx[b] = total.astype(BF16)
+        ctx[b, span, :] = total.astype(BF16)
 
     step = wide(dim)
 
     def project(layer, source, weight, lo, hi):
-        span = pl.ds(lo * rows, (hi - lo) * rows)
-        left = source[other, span, :]
+        count = (hi - lo) * rows
+        span = pl.ds(lo * rows, count)
+        both = full([source[other, span, :], source[core, span, :]], axis=0)
 
         @pl.loop(0, dim // step)
         def _(j):
             at = pl.ds(pl.multiple_of(j * step, step), step)
-            sib_out[layer, span, at] = dot(left, weight[:, at]).astype(BF16)
+            part = dot(both, weight[:, at])
+            sib_out[layer, span, at] = part[:count].astype(BF16)
+            acc[span, at] = part[count:]
 
         copies = []
         for r in range(lo, hi):
@@ -312,15 +312,6 @@
             )
         return copies
 
-    def own(source, weight, lo, hi):
-        span = pl.ds(lo * rows, (hi - lo) * rows)
-        right = source[core, span, :]
-
-        @pl.loop(0, dim // step)
-        def _(j):
-            at = pl.ds(pl.multiple_of(j * step, step), step)
-            acc[span, at] = dot(right, weight[:, at])
-
     def cross(layer, near, lo, hi):
         copies = []
         for r in range(lo, hi):
@@ -351,65 +342,88 @@
         pending.extend(copies)
         return copies
 
-    attend(other)
+    group = CHUNKS // 2
     loads[1].wait()
-    near = project(0, ctx, wo, 0, CHUNKS)
-    attend(core)
-    own(ctx, wo, 0, CHUNKS)
-    across0 = cross(0, near, 0, CHUNKS)
+    across0 = []
+    for b in range(2):
+        attend(b, 0, CHUNKS)
+    for lo in range(0, CHUNKS, group):
+        near = project(0, ctx, wo, lo, lo + group)
+        across0 += cross(0, near, lo, lo + group)
+
+    for copy in ints_copies[1:]:
+        copy.wait_recv()
+    slots_here = out_ref.shape[0]
+    want = lax.broadcasted_iota(jnp.int32, (slots_here, 128), 0)
+    lanes = lax.broadcasted_iota(jnp.int32, (slots_here, 128), 1)
+    index = jnp.zeros((slots_here, 128), jnp.int32)
+    for k in range(ranks):
+        hit = (want == ints_in[k, pl.ds(me, 1), :]) & (lanes < cap)
+        index = index + jnp.where(hit, k * cap + lanes + 1, 0)
+    index = jnp.sum(index, axis=1, keepdims=True) - 1
+    source_v[...] = jnp.broadcast_to(index, (slots_here, 128))
+    to_scalar.append(pltpu.make_async_copy(source_v, source_s, s_sem.at[0]))
+    to_scalar[1].start()
+
+    loads[4].wait()
+    kv_half = wkv_raw.shape[2]
+
+    @pl.loop(0, wkv_raw.shape[0] // 64)
+    def _(i):
+        at = pl.ds(pl.multiple_of(i * 64, 64), 64)
+        block = wkv_raw[at].astype(F32)
+        wkv[at, 0:kv_half] = block[:, 0, :].astype(BF16)
+        wkv[at, kv_half:] = block[:, 1, :].astype(BF16)
 
     loads[2].wait()
     loads[3].wait()
     ff = w1.shape[1]
     ff_step = wide(ff)
-    group = CHUNKS // 2
-
-    def up(b, lo, hi):
-        span = pl.ds(lo * rows, (hi - lo) * rows)
-        act = n2[b, span, :]
+
+    def up(lo, hi):
+        count = (hi - lo) * rows
+        span = pl.ds(lo * rows, count)
+        act = n2[:, span, :].reshape(2 * count, dim)
 
         @pl.loop(0, ff // ff_step)
         def _(j):
             at = pl.ds(pl.multiple_of(j * ff_step, ff_step), ff_step)
             inner = dot(act, w1[:, at]) + fb1_ref[:, at]
             gelu = inner * (1.0 + lax.erf(inner * (0.5**0.5))) * 0.5
-            hid[b, span, at] = gelu.astype(BF16)
+            hid[:, span, at] = gelu.astype(BF16).reshape(2, count, ff_step)
 
     across1 = []
     for lo in range(0, CHUNKS, group):
         hi = lo + group
         came = settle(0, across0, lo, hi, g2, b2, 0.0, n2)
-        up(core, lo, hi)
         for copy in came:
             copy.wait_recv()
-        up(other, lo, hi)
+        up(lo, hi)
         near = project(1, hid, w2, lo, hi)
-        own(hid, w2, lo, hi)
         across1 += cross(1, near, lo, hi)
 
-    loads[4].wait()
     half = wkv.shape[1] // 2
 
-    def pages(b, lo, hi):
+    def pages(lo, hi):
         count = (hi - lo) * rows
-        both = dot(n3[b, pl.ds(lo * rows, count), :], wkv[...])
+        both = dot(n3[:, pl.ds(lo * rows, count), :].reshape(2 * count, dim), wkv[...])
         parts = []
         for h in range(half // KV_DIM):
             key = both[:, h * KV_DIM : (h + 1) * KV_DIM]
             size = jnp.mean(key * key, axis=-1, keepdims=True)
             parts.append(key * lax.rsqrt(size + 1e-05) * kg_ref[...])
         parts.append(both[:, half:])
-        joined = full(parts, axis=1)
-        first = b * (length // PAGE) + lo * rows // PAGE
-        kvp[pl.ds(first, count // PAGE)] = joined.reshape(count // PAGE, PAGE, 2 * half).astype(BF16)
+        joined = full(parts, axis=1).reshape(2, count // PAGE, PAGE, 2 * half).astype(BF16)
+        for b in range(2):
+            first = b * (length // PAGE) + lo * rows // PAGE
+            kvp[pl.ds(first, count // PAGE)] = joined[b]
 
     for lo in range(0, CHUNKS, group):
         hi = lo + group
         came = settle(1, across1, lo, hi, g3, b3, fb2[...], n3)
-        pages(core, lo, hi)
         for copy in came:
             copy.wait_recv()
-        pages(other, lo, hi)
+        pages(lo, hi)
 
     for copy in to_scalar:
         copy.wait()
@@ -475,7 +489,6 @@
     local = qkv_weight.shape[2]
     ff = fc1_weight.shape[1]
     kv_cols = 2 * kv_weight.shape[2]
-    wkv = kv_weight.reshape(dim, kv_cols)
     vmem = pl.BlockSpec(memory_space=pltpu.VMEM)
     smem = pl.BlockSpec(memory_space=pltpu.SMEM)
     anywhere = pl.BlockSpec(memory_space=pl.ANY)
@@ -495,10 +508,13 @@
             pltpu.VMEM((local, dim), BF16),
             pltpu.VMEM((dim, ff), BF16),
             pltpu.VMEM((ff, dim), BF16),
+            pltpu.VMEM(kv_weight.shape, BF16),
             pltpu.VMEM((dim, kv_cols), BF16),
             pltpu.VMEM((shards, dim // shards, patch), BF16),
-            pltpu.VMEM((owner_rows + 8, 128), jnp.int32),
-            pltpu.VMEM((ranks, owner_rows + 8, 128), jnp.int32),
+            pltpu.VMEM((owner_rows, 128), jnp.int32),
+            pltpu.VMEM((ranks, owner_rows, 128), jnp.int32),
+            pltpu.VMEM((8, 128), jnp.int32),
+            pltpu.VMEM((ranks, 8, 128), jnp.int32),
             pltpu.VMEM((owner_rows, 128), jnp.int32),
             pltpu.SMEM((owner_rows, 128), jnp.int32),
             pltpu.VMEM((8, dim), F32),
@@ -526,6 +542,7 @@
             pltpu.VMEM((cache_slots, 128), jnp.int32),
             pltpu.SMEM((cache_slots, 128), jnp.int32),
             pltpu.SemaphoreType.DMA((5,)),
+            sems(ranks),
             sems(ranks),
             sems(ranks),
             sems(ranks),
@@ -561,7 +578,7 @@
         out_weight,
         fc1_weight,
         fc2_weight,
-        wkv,
+        kv_weight,
     )
     return cache.reshape(cache_slots, PAGE, 2, kv_cols // 2)
 

time: 94.9 us -> 90.9 us (0.958)
  local copies, waits for them, and re-layouts: 4.79 us -> 2.14 us
    unnamed x1 -> x0, local copies, waits for them, and re-layouts: 2.65 us -> none
where the time goes in v3:
time: 90.9 us; the launch traced here: 90.3 us
  Pallas kernels  88.1 us (97%)
  local copies, waits for them, and re-layouts  2.14 us (2%)
    pallas_call x1, Pallas kernels, on_device(): pl.pallas_call(functools.partial(kernel, ranks, cap), out_shape=jax.Shape...  88.1 us
    reshape x1, local copies, waits for them, and re-layouts, on_device(): return cache.reshape(cache_slots, PAGE, 2, kv_cols // 2)  2.14 us

profile of v3, /device:TPU:15, one launch (start us, length us, event | category | flops | bytes accessed | tf_op | source)
XLA Modules:
  0.0 90.3 jit_solution(10993987348361652802)
XLA Ops:
  0.0 88.1 %encoder.1 = bf16[64,16,512]{2,1,0:T(8,128)(2,1)} custom-call(s32[8]{0:T(128)} %from_ref.1, s32[4]{0:T(128)} %position_ref.1, s32[32]{0:T(128)} %owner_ref.1, s32[32]{0:T(128)} %slot_ref.1, bf16[4,64,588]{2,1,0:T(8,128)(2,1)} %tiles_ref.1, bf16[320,588]{1,0:T(8,128)(2,1)} %bitcast.4, f32[4,1280]{1,0:T(4,128)} %table_ref.1, f32[1280]{0:T(1024)} %g1_in.1, ...), custom_call_target="tpu_custom_call" | custom-call | tf_op jit(solution)/shard_map/encoder/pallas_call | solution.py:501
  88.1 2.1 %reshape.3 = bf16[64,16,2,256]{3,2,1,0:T(2,128)(2,1)} reshape(bf16[64,16,512]{2,1,0:T(8,128)(2,1)} %encoder.1) | data formatting | bytes 2097152 | tf_op jit(solution)/shard_map/reshape | solution.py:583
